TPU v7x, 32 devices: a whole 2x2x4 slice. The times are simulated.
32 devices in a mesh: groups: 2 (over x), row: 16 (over z, y, core).
Axes of the slice: x: 2, y: 2, z: 4, core: 2. Of those that a mesh axis runs over, the one named last changes fastest.
Arguments:
- alignment_features: bfloat16 [64, 128, 64], P(('groups', 'row')), parts along dimension 0
- pair_features: bfloat16 [256, 128, 128], P(('groups', 'row')), parts along dimension 0
- token_residue_kind: int32 [256], P('groups'), parts along dimension 0, may hold values from 0 to 31
- alignment_mask: int32 [64], P('groups'), parts along dimension 0, may hold values from 0 to 1, as said below
- residue_embedding_table: bfloat16 [32, 64], replicated, may hold values from -0.099609375 to 0.099609375
- outer_left_weight: bfloat16 [64, 32], replicated, may hold values from -0.75 to 0.75
- outer_right_weight: bfloat16 [64, 32], replicated, may hold values from -0.75 to 0.75
- outer_output_weight: bfloat16 [1024, 128], replicated
- averaging_value_weight: bfloat16 [64, 256], replicated, may hold values from -0.75 to 0.75
- averaging_gate_weight: bfloat16 [64, 256], replicated, may hold values from -0.75 to 0.75
- averaging_head_logits: bfloat16 [128, 8], replicated
- averaging_output_weight: bfloat16 [256, 64], replicated, may hold values from -0.375 to 0.375
- triangle_projection_weight: bfloat16 [128, 512], replicated, may hold values from -0.5 to 0.5
- triangle_gate_weight: bfloat16 [128, 128], replicated, may hold values from -0.5 to 0.5
- triangle_output_weight: bfloat16 [128, 128], replicated, may hold values from -1.5 to 1.5
Outputs:
- alignment_output: bfloat16 [64, 128, 64], P(('groups', 'row')), parts along dimension 0
- pair_output: bfloat16 [256, 128, 128], P(('groups', 'row')), parts along dimension 0
There are 2 independent parts, one for each index of `groups`. A program takes and returns all parts, laid end to end along the dimension named above; an argument that names none is the same for every part. Nothing has to cross between parts.
Inputs may be any that keep to these rules, and one draw needn't show every extreme that they name: `alignment_mask`: the first sequence is always valid.
All inputs are finite; a program needn't handle non-finite values.
Results may differ from a plain program's by a relative error of at most 0.038.
Values may be sent and summed in bfloat16 or wider, within the bound.
A program may use at most 64 MiB of HBM per device.

v0:
```python
import jax
import jax.numpy as jnp
from jax import lax
from jax.sharding import PartitionSpec as P


def layer_normalize(inputs, axis):
    average = jnp.mean(inputs, axis=axis, keepdims=True)
    centered = inputs - average
    variance = jnp.mean(centered * centered, axis=axis, keepdims=True)
    return centered * lax.rsqrt(variance + 1e-05)


def local(
    alignment_features,
    pair_features,
    token_residue_kind,
    alignment_mask,
    residue_embedding_table,
    outer_left_weight,
    outer_right_weight,
    outer_output_weight,
    averaging_value_weight,
    averaging_gate_weight,
    averaging_head_logits,
    averaging_output_weight,
    triangle_projection_weight,
    triangle_gate_weight,
    triangle_output_weight,
):
    tok_dev = pair_features.shape[0]
    all_tokens = pair_features.shape[1]
    sequences_per_shard = alignment_features.shape[0]
    width = outer_left_weight.shape[1]
    heads = averaging_head_logits.shape[1]
    channels = triangle_output_weight.shape[0]
    classes = residue_embedding_table.shape[0]
    one_hot = (token_residue_kind[:, None] == jnp.arange(classes, dtype=jnp.int32)[None, :]).astype(
        jnp.bfloat16
    )
    embedded_input = jnp.dot(one_hot, residue_embedding_table, preferred_element_type=jnp.float32)
    alignment_start = (alignment_features.astype(jnp.float32) + embedded_input[None]).astype(
        jnp.bfloat16
    )
    alignment_normalized = layer_normalize(alignment_start.astype(jnp.float32), 2).astype(
        jnp.bfloat16
    )
    mask_as_float = alignment_mask.astype(jnp.float32)
    own_mask = lax.dynamic_slice_in_dim(
        mask_as_float, lax.axis_index("row") * sequences_per_shard, sequences_per_shard, 0
    )
    left_projected_rows = (
        jnp.dot(alignment_normalized, outer_left_weight, preferred_element_type=jnp.float32)
        * own_mask[:, None, None]
    ).astype(jnp.bfloat16)
    right_projected_rows = jnp.dot(
        alignment_normalized, outer_right_weight, preferred_element_type=jnp.float32
    ).astype(jnp.bfloat16)
    seq_count = jnp.sum(mask_as_float)
    left_all, right_all = (
        lax.all_gather(left_projected_rows, "row", axis=0, tiled=True),
        lax.all_gather(right_projected_rows, "row", axis=0, tiled=True),
    )
    left_mine = lax.dynamic_slice_in_dim(left_all, lax.axis_index("row") * tok_dev, tok_dev, 1)
    right_flat = right_all.reshape(right_all.shape[0], all_tokens * width)
    opm_weight = outer_output_weight.reshape(width, width, -1)

    def outer_block(left_row):
        summed = jnp.dot(left_row.T, right_flat, preferred_element_type=jnp.float32)
        product = (summed / seq_count).astype(jnp.bfloat16).reshape(width, all_tokens, width)
        return jnp.einsum("ajb,abk->jk", product, opm_weight, preferred_element_type=jnp.float32)

    opm_update = lax.map(outer_block, jnp.swapaxes(left_mine, 0, 1))
    pair_mid = (pair_features.astype(jnp.float32) + opm_update).astype(jnp.bfloat16)
    pair_normed = layer_normalize(pair_mid.astype(jnp.float32), 2).astype(jnp.bfloat16)
    logits = jnp.einsum(
        "ijc,ch->hij", pair_normed, averaging_head_logits, preferred_element_type=jnp.float32
    )
    weights = jax.nn.softmax(logits, axis=2).astype(jnp.bfloat16)
    value_rows = jnp.dot(
        alignment_normalized, averaging_value_weight, preferred_element_type=jnp.float32
    ).astype(jnp.bfloat16)
    value_rows = value_rows.reshape(sequences_per_shard, all_tokens, heads, -1)
    weight_rows = lax.all_gather(weights, "row", axis=1, tiled=True)
    result = jnp.einsum(
        "hij,sjhd->sihd", weight_rows, value_rows, preferred_element_type=jnp.float32
    )
    averaged = result.reshape(sequences_per_shard, weight_rows.shape[1], -1)
    gating_values = jax.nn.sigmoid(
        jnp.dot(alignment_normalized, averaging_gate_weight, preferred_element_type=jnp.float32)
    )
    gated_output = (gating_values * averaged).astype(jnp.bfloat16)
    alignment_output = (
        alignment_start.astype(jnp.float32)
        + jnp.dot(gated_output, averaging_output_weight, preferred_element_type=jnp.float32)
    ).astype(jnp.bfloat16)
    projected = [
        jnp.einsum(
            "ijc,ce->eij",
            pair_normed,
            triangle_projection_weight[:, column_block * channels : (column_block + 1) * channels],
            preferred_element_type=jnp.float32,
        )
        for column_block in range(4)
    ]
    tri_left = (jax.nn.sigmoid(projected[1]) * projected[0]).astype(jnp.bfloat16)
    tri_right = (jax.nn.sigmoid(projected[3]) * projected[2]).astype(jnp.bfloat16)
    owned_left, owned_right = (
        lax.all_to_all(tri_left, "row", split_axis=0, concat_axis=1, tiled=True),
        lax.all_to_all(tri_right, "row", split_axis=0, concat_axis=1, tiled=True),
    )
    tri_sum = jnp.einsum(
        "cik,cjk->cij", owned_left, owned_right, preferred_element_type=jnp.float32
    ).astype(jnp.bfloat16)
    back_rows = lax.all_to_all(tri_sum, "row", split_axis=1, concat_axis=0, tiled=True)
    tri_normed = layer_normalize(back_rows.astype(jnp.float32), 0).astype(jnp.bfloat16)
    tri_update = jnp.einsum(
        "cij,cz->ijz", tri_normed, triangle_output_weight, preferred_element_type=jnp.float32
    )
    tri_gate = jax.nn.sigmoid(
        jnp.dot(pair_normed, triangle_gate_weight, preferred_element_type=jnp.float32)
    )
    pair_output = (pair_mid.astype(jnp.float32) + tri_gate * tri_update).astype(jnp.bfloat16)
    return (alignment_output, pair_output)


def solution(mesh):
    placed = (
        P(("groups", "row"), None, None),
        P(("groups", "row"), None, None),
        P("groups"),
        P("groups"),
        P(),
        P(),
        P(),
        P(),
        P(),
        P(),
        P(),
        P(),
        P(),
        P(),
        P(),
    )
    return jax.shard_map(
        local,
        mesh=mesh,
        in_specs=placed,
        out_specs=(P(("groups", "row"), None, None), P(("groups", "row"), None, None)),
        check_vma=False,
    )
```

profile of v0, /device:TPU:0, one launch (start us, length us, event | category | flops | bytes accessed | tf_op | source)
XLA Modules:
  0.0 126.0 jit_solution(12356332115103515872)
XLA Ops:
  1.9 0.9 fusion.54
  3.7 23.8 %all_gather.9 = bf16[32,128,32]{1,2,0:T(8,128)(2,1)S(1)} all-gather(bf16[2,128,32]{1,2,0:T(8,128)(2,1)S(1)} %fusion.33), channel_id=1, replica_groups=mesh['groups'=2,'row'=16] {'row'}, dimensions={0}, use_global_device_ids=true | all-gather | bytes 278528 | tf_op jit(solution)/shard_map/all_gather | solution.py:61
  28.5 18.1 %all_gather.10 = bf16[32,128,32]{1,2,0:T(8,128)(2,1)S(1)} all-gather(bf16[2,128,32]{1,2,0:T(8,128)(2,1)S(1)} %convolution_convert_fusion.2), channel_id=1, replica_groups=mesh['groups'=2,'row'=16] {'row'}, dimensions={0}, use_global_device_ids=true | all-gather | bytes 278528 | tf_op jit(solution)/shard_map/all_gather | solution.py:62
  47.1 1.1 reshape.67
  48.3 16.9 %while.10 = (s32[]{:T(128)}, f32[8,128,128]{2,1,0:T(8,128)S(1)}, bf16[8,32,32]{2,1,0:T(8,128)(2,1)S(1)}, bf16[32,4096]{1,0:T(8,128)(2,1)S(1)}, f32[]{:T(128)}, /*index=5*/bf16[32,32,128]{2,1,0:T(8,128)(2,1)S(1)}, s32[]{:T(128)}) while((s32[]{:T(128)}, f32[8,128,128]{2,1,0:T(8,128)S(1)}, bf16[8,32,32]{2,1,0:T(8,128)(2,1)S(1)}, ...), condition=%wide.region_4.5_spmd, body=%wide.region_3.4_spmd.sunk | while | flops 42205184 | bytes 2433113 | solution.py:73
  48.3 0.9 fusion.107
  50.4 0.9 fusion.107
  52.5 0.9 fusion.107
  54.7 0.9 fusion.107
  56.8 0.9 fusion.107
  58.9 0.9 fusion.107
  61.0 0.9 fusion.107
  63.1 0.9 fusion.107
  67.2 0.9 copy.60
  68.1 3.5 %all-to-all-start = ((bf16[128,8,128]{2,1,0:T(8,128)(2,1)}), bf16[128,8,128]{2,1,0:T(8,128)(2,1)S(1)}, u32[]{:S(2)}, u32[]{:S(2)}) async-start(bf16[128,8,128]{2,1,0:T(8,128)(2,1)} %copy.60), calls=%async_computation | async-start | bytes 524288 | tf_op jit(solution)/shard_map/all_to_all | solution.py:109
  72.6 0.9 copy.62
  73.5 8.2 %all-to-all-done = bf16[128,8,128]{2,1,0:T(8,128)(2,1)S(1)} async-done(((bf16[128,8,128]{2,1,0:T(8,128)(2,1)}), bf16[128,8,128]{2,1,0:T(8,128)(2,1)S(1)}, u32[]{:S(2)}, u32[]{:S(2)}) %all-to-all-start) | async-done | bytes 262176 | tf_op jit(solution)/shard_map/all_to_all | solution.py:109
  81.7 3.5 %all-to-all-start.1 = ((bf16[128,8,128]{2,1,0:T(8,128)(2,1)}), bf16[128,8,128]{2,1,0:T(8,128)(2,1)S(1)}, u32[]{:S(2)}, u32[]{:S(2)}) async-start(bf16[128,8,128]{2,1,0:T(8,128)(2,1)} %copy.62), calls=%async_computation.1 | async-start | bytes 524288 | tf_op jit(solution)/shard_map/all_to_all | solution.py:110
  86.7 22.4 %all_gather.11 = bf16[8,128,128]{2,0,1:T(8,128)(2,1)S(1)} all-gather(bf16[8,8,128]{2,0,1:T(8,128)(2,1)S(1)} %fusion.34), channel_id=1, replica_groups=mesh['groups'=2,'row'=16] {'row'}, dimensions={1}, use_global_device_ids=true | all-gather | bytes 278528 | tf_op jit(solution)/shard_map/all_gather | solution.py:84
  109.4 0.9 copy.64
  110.3 3.5 %all-to-all-start.2 = ((bf16[8,128,128]{2,0,1:T(8,128)(2,1)}), bf16[8,128,128]{2,0,1:T(8,128)(2,1)S(1)}, u32[]{:S(2)}, u32[]{:S(2)}) async-start(bf16[8,128,128]{2,0,1:T(8,128)(2,1)} %copy.64), calls=%async_computation.2 | async-start | bytes 524288 | tf_op jit(solution)/shard_map/all_to_all | solution.py:115
  114.9 1.0 fusion.29
  116.6 7.2 %all-to-all-done.2 = bf16[8,128,128]{2,0,1:T(8,128)(2,1)S(1)} async-done(((bf16[8,128,128]{2,0,1:T(8,128)(2,1)}), bf16[8,128,128]{2,0,1:T(8,128)(2,1)S(1)}, u32[]{:S(2)}, u32[]{:S(2)}) %all-to-all-start.2) | async-done | bytes 262176 | tf_op jit(solution)/shard_map/all_to_all | solution.py:115
  125.0 1.0 fusion.17
  (81 shorter events, 20.5 us)
Async XLA Ops:
  0.6 115.3 %copy-start = (bf16[128,128]{1,0:T(8,128)(2,1)S(1)}, bf16[128,128]{1,0:T(8,128)(2,1)}, u32[]{:S(2)}) copy-start(bf16[128,128]{1,0:T(8,128)(2,1)} %param.30) | copy-start | bytes 98308
  0.6 0.7 copy-start.12
  0.7 1.3 copy-start.13
  1.3 1.5 %copy-start.4 = (bf16[2,128,64]{1,2,0:T(8,128)(2,1)S(1)}, bf16[2,128,64]{1,2,0:T(8,128)(2,1)}, u32[]{:S(2)}) copy-start(bf16[2,128,64]{1,2,0:T(8,128)(2,1)} %param.17) | copy-start | bytes 98308
  2.9 0.7 copy-start.10
  27.7 0.7 copy-start.7
  47.1 1.1 copy-start.1
  48.3 16.9 %copy-start.2 = (bf16[8,128,128]{2,1,0:T(8,128)(2,1)S(1)}, bf16[8,128,128]{2,1,0:T(8,128)(2,1)}, u32[]{:S(2)}) copy-start(bf16[8,128,128]{2,1,0:T(8,128)(2,1)} %param.18) | copy-start | bytes 786436
  65.4 0.9 copy-start.3
  68.1 13.5 %all-to-all-start = ((bf16[128,8,128]{2,1,0:T(8,128)(2,1)}), bf16[128,8,128]{2,1,0:T(8,128)(2,1)S(1)}, u32[]{:S(2)}, u32[]{:S(2)}) async-start(bf16[128,8,128]{2,1,0:T(8,128)(2,1)} %copy.60), calls=%async_computation | async-start | bytes 524288 | tf_op jit(solution)/shard_map/all_to_all | solution.py:109
  73.5 11.7 %copy-start.5 = (bf16[64,256]{1,0:T(8,128)(2,1)S(1)}, bf16[64,256]{1,0:T(8,128)(2,1)}, u32[]{:S(2)}) copy-start(bf16[64,256]{1,0:T(8,128)(2,1)} %param.25) | copy-start | bytes 98308
  81.7 27.4 %all-to-all-start.1 = ((bf16[128,8,128]{2,1,0:T(8,128)(2,1)}), bf16[128,8,128]{2,1,0:T(8,128)(2,1)S(1)}, u32[]{:S(2)}, u32[]{:S(2)}) async-start(bf16[128,8,128]{2,1,0:T(8,128)(2,1)} %copy.62), calls=%async_computation.1 | async-start | bytes 524288 | tf_op jit(solution)/shard_map/all_to_all | solution.py:110
  85.4 0.7 copy-start.11
  110.3 13.5 %all-to-all-start.2 = ((bf16[8,128,128]{2,0,1:T(8,128)(2,1)}), bf16[8,128,128]{2,0,1:T(8,128)(2,1)S(1)}, u32[]{:S(2)}, u32[]{:S(2)}) async-start(bf16[8,128,128]{2,0,1:T(8,128)(2,1)} %copy.64), calls=%async_computation.2 | async-start | bytes 524288 | tf_op jit(solution)/shard_map/all_to_all | solution.py:115
  114.1 0.8 copy-start.8
  114.2 0.8 copy-start.9
  124.2 0.8 copy-start.6
where the time goes:
time: 127 us; the launch traced here: 126 us
  blocking collectives  64.3 us (51%)
  matrix products  17.2 us (14%)
  local copies, waits for them, and re-layouts  15.5 us (12%)
  waiting for transfers between devices  15.4 us (12%)
  starting transfers between devices  10.6 us (8%)
  other arithmetic  1.67 us (1%)
    all_gather x1, blocking collectives, local(): lax.all_gather(left_projected_rows, 'row', axis=0, tiled=True)  23.8 us
    all_gather x1, blocking collectives, local(): weight_rows = lax.all_gather(weights, 'row', axis=1, tiled=True)  22.4 us
    all_gather x1, blocking collectives, local(): lax.all_gather(right_projected_rows, 'row', axis=0, tiled=True)  18.1 us
    all_to_all x1, waiting for transfers between devices, local(): lax.all_to_all(tri_left, 'row', split_axis=0, concat_axis=1, tiled=True)  8.18 us
    dot_general x8, matrix products, outer_block(): summed = jnp.dot(left_row.T, right_flat, preferred_element_type=jnp.float32)  7.23 us
    all_to_all x1, waiting for transfers between devices, local(): lax.all_to_all(tri_sum, 'row', split_axis=1, concat_axis=0, tiled=True)  7.2 us
    reshape x8, local copies, waits for them, and re-layouts, outer_block(): (summed / seq_count).astype(jnp.bfloat16).reshape(width, all_tokens, width)  6.37 us
    unnamed x28, local copies, waits for them, and re-layouts  4.17 us
  transfers between devices with their start and end apart: 3, of which 2 were waited for; matrix products, arithmetic and copies ran while one was open for 4% of the time, Pallas kernels for 0%

commit v1 on v0

--- a/solution.py
+++ b/solution.py
@@ -1,6 +1,10 @@
+import functools
+
 import jax
 import jax.numpy as jnp
 from jax import lax
+from jax.experimental import pallas as pl
+from jax.experimental.pallas import tpu as pltpu
 from jax.sharding import PartitionSpec as P
 
 
@@ -11,7 +15,7 @@
     return centered * lax.rsqrt(variance + 1e-05)
 
 
-def local(
+def local_large(
     alignment_features,
     pair_features,
     token_residue_kind,
@@ -124,6 +128,377 @@
     return (alignment_output, pair_output)
 
 
+F32 = jnp.float32
+BF16 = jnp.bfloat16
+
+
+def matmul(a, b, dim_a, dim_b):
+    return lax.dot_general(a, b, (((dim_a,), (dim_b,)), ((), ())), preferred_element_type=F32)
+
+
+def fused_kernel(
+    ranks,
+    msa_ref,
+    pair_hbm,
+    kind_ref,
+    mask_ref,
+    table_ref,
+    left_w_ref,
+    right_w_ref,
+    outer_w_hbm,
+    value_w_ref,
+    gate_w_ref,
+    head_w_ref,
+    average_w_ref,
+    tri_w_ref,
+    tri_gate_w_ref,
+    tri_out_w_ref,
+    msa_out_ref,
+    pair_out_ref,
+    pair_ref,
+    outer_w_ref,
+    outer_f32,
+    left_send,
+    left_buf,
+    right_buf,
+    right_f32,
+    right_all,
+    left_w_all,
+    pair_mid_ref,
+    pair_normed_ref,
+    weight_buf,
+    weight_f32,
+    tri_send,
+    tri_buf,
+    tri_f32,
+    back_send,
+    back_buf,
+    back_f32,
+    local_sem,
+    send_sem,
+    recv_sem,
+):
+    me = lax.axis_index("row")
+    seqs, channels, tokens = msa_ref.shape
+    rows = pair_ref.shape[0]
+    width = left_w_ref.shape[0]
+    heads = head_w_ref.shape[0]
+    pair_channels = tri_out_w_ref.shape[1]
+    tri_channels = tri_out_w_ref.shape[0]
+    owned = tri_channels // ranks
+    head_dim = value_w_ref.shape[1] // heads
+    sequences = seqs * ranks
+
+    load_pair = pltpu.make_async_copy(pair_hbm, pair_ref, local_sem.at[0])
+    load_outer = pltpu.make_async_copy(outer_w_hbm, outer_w_ref, local_sem.at[1])
+    load_outer.start()
+    load_pair.start()
+
+    barrier = pltpu.get_barrier_semaphore()
+
+    def greet(step, carry):
+        pl.semaphore_signal(
+            barrier,
+            inc=1,
+            device_id={"row": lax.rem(me + step, ranks)},
+            device_id_type=pl.DeviceIdType.MESH,
+        )
+        return carry
+
+    lax.fori_loop(1, ranks, greet, 0)
+
+    def remote(phase, step, source, target):
+        peer = lax.rem(me + step, ranks)
+        return pltpu.make_async_remote_copy(
+            src_ref=source.at[peer] if source is not target else source.at[me],
+            dst_ref=target.at[me],
+            send_sem=send_sem.at[phase, step],
+            recv_sem=recv_sem.at[phase, step],
+            device_id={"row": peer},
+            device_id_type=pl.DeviceIdType.MESH,
+        )
+
+    def send_all(phase, source, target):
+        def body(step, carry):
+            remote(phase, step, source, target).start()
+            return carry
+
+        lax.fori_loop(1, ranks, body, 0)
+
+    def receive_all(phase, source, target, wide):
+        def body(step, carry):
+            remote(phase, step, source, target).wait_recv()
+            if wide is not None:
+                origin = lax.rem(me - step + ranks, ranks)
+                wide[origin] = target[origin].astype(F32).reshape(wide.shape[1:])
+            return carry
+
+        lax.fori_loop(1, ranks, body, 0)
+
+    def drain(phase, source, target):
+        def body(step, carry):
+            remote(phase, step, source, target).wait_send()
+            return carry
+
+        lax.fori_loop(1, ranks, body, 0)
+
+    classes = table_ref.shape[0]
+    one_hot = jnp.where(
+        lax.broadcasted_iota(jnp.int32, (classes, tokens), 0) == kind_ref[...], 1.0, 0.0
+    ).astype(BF16)
+    embedded = matmul(table_ref[...], one_hot, 0, 0)
+    mask = mask_ref[...].astype(F32)
+    seq_count = jnp.sum(mask, axis=1, keepdims=True)
+    lane = lax.broadcasted_iota(jnp.int32, mask.shape, 1)
+    starts = []
+    normed = []
+    for s in range(seqs):
+        start = (msa_ref[s].astype(F32) + embedded).astype(BF16)
+        starts.append(start)
+        normed.append(layer_normalize(start.astype(F32), 0).astype(BF16))
+    msa_normed = jnp.concatenate(normed, axis=1)
+    right = matmul(right_w_ref[...], msa_normed, 1, 0).astype(BF16)
+    left = matmul(left_w_ref[...], msa_normed, 1, 0)
+    left_rows = []
+    for s in range(seqs):
+        own = jnp.sum(jnp.where(lane == me * seqs + s, mask, 0.0), axis=1, keepdims=True)
+        part = slice(s * tokens, (s + 1) * tokens)
+        right_buf[me, s * width : (s + 1) * width] = right[:, part]
+        left_rows.append((left[:, part] * own).astype(BF16).astype(F32))
+    left_rows.append(jnp.zeros((128 - seqs * width, tokens), F32))
+    left_turned = jnp.concatenate(left_rows, axis=0).T
+    left_send[...] = left_turned.reshape(ranks, rows, 128)
+
+    pl.semaphore_wait(barrier, ranks - 1)
+    send_all(0, right_buf, right_buf)
+    send_all(1, left_send, left_buf)
+
+    left_buf[me] = left_send[me]
+    right_f32[me] = right_buf[me].astype(F32)
+    load_outer.wait()
+    outer_f32[...] = outer_w_ref[...].astype(F32)
+    turned = tri_w_ref[...].astype(F32).T
+    blocks = [
+        turned[n * tri_channels : (n + 1) * tri_channels].reshape(ranks, owned, pair_channels)
+        for n in range(4)
+    ]
+    project_w = jnp.concatenate([blocks[0], blocks[2]], axis=1).reshape(-1, pair_channels)
+    sigmoid_w = jnp.concatenate([blocks[1], blocks[3]], axis=1).reshape(-1, pair_channels)
+    tri_w = jnp.concatenate([project_w, sigmoid_w], axis=0).astype(BF16)
+    values = matmul(value_w_ref[...], msa_normed, 0, 0).astype(BF16)
+    gates = jax.nn.sigmoid(matmul(gate_w_ref[...], msa_normed, 0, 0))
+
+    receive_all(1, left_send, left_buf, None)
+    left_lane = lax.broadcasted_iota(jnp.int32, (ranks, seqs * width), 1)
+    left_parts = []
+    for i in range(rows):
+        one = left_buf.reshape(ranks * rows, 128)[pl.ds(i, ranks, stride=rows), :][:, : seqs * width]
+        for s in range(seqs):
+            keep = (left_lane >= s * width) & (left_lane < (s + 1) * width)
+            left_parts.append(jnp.where(keep, one, 0.0))
+    left_all = jnp.concatenate(left_parts, axis=0).astype(BF16)
+    for b in range(0, width, 2):
+        pieces = [
+            outer_f32[pl.ds(b + n, width, stride=width), :].astype(BF16) for n in range(2)
+        ]
+        both = jnp.concatenate(pieces, axis=1)
+        product = matmul(left_all, jnp.concatenate([both] * seqs, axis=0), 1, 0).astype(BF16)
+        for n in range(2):
+            for i in range(rows):
+                left_w_all[
+                    (b + n) * sequences : (b + n + 1) * sequences,
+                    i * pair_channels : (i + 1) * pair_channels,
+                ] = product[
+                    i * sequences : (i + 1) * sequences,
+                    n * pair_channels : (n + 1) * pair_channels,
+                ]
+
+    receive_all(0, right_buf, right_buf, right_f32)
+    right_flat = right_f32.reshape(ranks * seqs * width, tokens)
+    for b in range(width):
+        parts = [
+            right_flat[pl.ds(s * width + b, ranks, stride=seqs * width), :] for s in range(seqs)
+        ]
+        right_all[b * sequences : (b + 1) * sequences] = jnp.concatenate(parts, axis=0).astype(BF16)
+    load_pair.wait()
+    scale = 1.0 / seq_count
+    right_turned = right_all[...].T
+    for i in range(0, rows, 2):
+        update = matmul(
+            right_turned, left_w_all[:, i * pair_channels : (i + 2) * pair_channels], 1, 0
+        )
+        for n in range(2):
+            mid = (
+                pair_ref[i + n].astype(F32)
+                + update[:, n * pair_channels : (n + 1) * pair_channels] * scale
+            ).astype(BF16)
+            pair_mid_ref[i + n] = mid
+            pair_normed_ref[i + n] = layer_normalize(mid.astype(F32), 1).astype(BF16)
+        pair_normed = pair_normed_ref[i : i + 2].reshape(2 * tokens, pair_channels)
+        projected = matmul(tri_w, pair_normed, 1, 1)
+        half = 2 * tri_channels
+        gated = (jax.nn.sigmoid(projected[half:]) * projected[:half]).astype(BF16)
+        for n in range(2):
+            tri_send[:, i + n] = gated[:, n * tokens : (n + 1) * tokens].reshape(
+                ranks, 2 * owned, tokens
+            )
+    send_all(2, tri_send, tri_buf)
+
+    pair_normed = pair_normed_ref[...].reshape(rows * tokens, pair_channels)
+    logits = matmul(head_w_ref[...], pair_normed, 1, 1)
+    logits = jnp.concatenate(
+        [logits[:, i * tokens : (i + 1) * tokens] for i in range(rows)], axis=0
+    )
+    powers = jnp.exp(logits - jnp.max(logits, axis=1, keepdims=True))
+    weight_buf[me] = (powers / jnp.sum(powers, axis=1, keepdims=True)).astype(BF16)
+    send_all(3, weight_buf, weight_buf)
+    weight_f32[me] = weight_buf[me].astype(F32)
+    tri_buf[me] = tri_send[me]
+    tri_f32[me] = tri_send[me].astype(F32).reshape(tri_f32.shape[1:])
+    tri_gate = jax.nn.sigmoid(matmul(pair_normed, tri_gate_w_ref[...], 1, 0))
+
+    receive_all(2, tri_send, tri_buf, tri_f32)
+    tri_flat = tri_f32.reshape(ranks * rows * 2 * owned, tokens)
+    sums = []
+    for c in range(owned):
+        sides = [
+            tri_flat[pl.ds(n * owned + c, tokens, stride=2 * owned), :].astype(BF16)
+            for n in range(2)
+        ]
+        sums.append(matmul(sides[0], sides[1], 1, 1).reshape(ranks, rows, tokens))
+        if c % 2 == 1:
+            back_send[:, (c - 1) * rows : (c + 1) * rows] = jnp.concatenate(
+                sums[-2:], axis=1
+            ).astype(BF16)
+    send_all(4, back_send, back_buf)
+    back_buf[me] = back_send[me]
+    back_f32[me] = back_send[me].astype(F32)
+
+    receive_all(3, weight_buf, weight_buf, weight_f32)
+    weight_flat = weight_f32.reshape(ranks * rows * heads, tokens)
+    averaged = [[] for _ in range(seqs)]
+    for h in range(heads):
+        weights = weight_flat[pl.ds(h, tokens, stride=heads), :].astype(BF16)
+        part = values[h * head_dim : (h + 1) * head_dim]
+        part = jnp.concatenate(
+            [part[:, s * tokens : (s + 1) * tokens] for s in range(seqs)], axis=0
+        )
+        result = matmul(part, weights, 1, 1)
+        for s in range(seqs):
+            averaged[s].append(result[s * head_dim : (s + 1) * head_dim])
+    gated = (
+        gates
+        * jnp.concatenate([jnp.concatenate(one, axis=0) for one in averaged], axis=1)
+    ).astype(BF16)
+    update = matmul(average_w_ref[...], gated, 1, 0)
+    for s in range(seqs):
+        msa_out_ref[s] = (
+            starts[s].astype(F32) + update[:, s * tokens : (s + 1) * tokens]
+        ).astype(BF16)
+
+    receive_all(4, back_send, back_buf, back_f32)
+    back_flat = back_f32.reshape(tri_channels * rows, tokens)
+    for i in range(rows):
+        one = back_flat[pl.ds(i, tri_channels, stride=rows), :]
+        tri_normed = layer_normalize(one, 0).astype(BF16)
+        update = matmul(tri_normed, tri_out_w_ref[...], 0, 0)
+        pair_out_ref[i] = (
+            pair_mid_ref[i].astype(F32) + tri_gate[i * tokens : (i + 1) * tokens] * update
+        ).astype(BF16)
+    drain(0, right_buf, right_buf)
+    drain(1, left_send, left_buf)
+    drain(2, tri_send, tri_buf)
+    drain(3, weight_buf, weight_buf)
+    drain(4, back_send, back_buf)
+
+
+def local(ranks, *arguments):
+    (
+        alignment_features,
+        pair_features,
+        token_residue_kind,
+        alignment_mask,
+        residue_embedding_table,
+        outer_left_weight,
+        outer_right_weight,
+        outer_output_weight,
+        averaging_value_weight,
+        averaging_gate_weight,
+        averaging_head_logits,
+        averaging_output_weight,
+        triangle_projection_weight,
+        triangle_gate_weight,
+        triangle_output_weight,
+    ) = arguments
+    seqs, tokens, channels = alignment_features.shape
+    rows, _, pair_channels = pair_features.shape
+    tri_channels = triangle_output_weight.shape[0]
+    width = outer_left_weight.shape[1]
+    heads = averaging_head_logits.shape[1]
+    owned = tri_channels // ranks
+    if (2 * owned) % 16 or rows != 8 or heads != 8 or (seqs * ranks) % 16 or seqs * width > 128:
+        return local_large(*arguments)
+    sequences = seqs * ranks
+    vmem = pl.BlockSpec(memory_space=pltpu.VMEM)
+    hbm = pl.BlockSpec(memory_space=pl.ANY)
+    in_specs = [vmem] * 15
+    in_specs[1] = hbm
+    in_specs[7] = hbm
+    msa_out, pair_out = pl.pallas_call(
+        functools.partial(fused_kernel, ranks),
+        out_shape=(
+            jax.ShapeDtypeStruct((seqs, channels, tokens), BF16),
+            jax.ShapeDtypeStruct((rows, tokens, pair_channels), BF16),
+        ),
+        in_specs=in_specs,
+        out_specs=(vmem, vmem),
+        scratch_shapes=[
+            pltpu.VMEM((rows, tokens, pair_channels), BF16),
+            pltpu.VMEM((width * width, pair_channels), BF16),
+            pltpu.VMEM((width * width, pair_channels), F32),
+            pltpu.VMEM((ranks, rows, 128), F32),
+            pltpu.VMEM((ranks, rows, 128), F32),
+            pltpu.VMEM((ranks, seqs * width, tokens), BF16),
+            pltpu.VMEM((ranks, seqs * width, tokens), F32),
+            pltpu.VMEM((width * sequences, tokens), BF16),
+            pltpu.VMEM((width * sequences, rows * pair_channels), BF16),
+            pltpu.VMEM((rows, tokens, pair_channels), BF16),
+            pltpu.VMEM((rows, tokens, pair_channels), BF16),
+            pltpu.VMEM((ranks, rows * heads, tokens), BF16),
+            pltpu.VMEM((ranks, rows * heads, tokens), F32),
+            pltpu.VMEM((ranks, rows, 2 * owned, tokens), BF16),
+            pltpu.VMEM((ranks, rows, 2 * owned, tokens), BF16),
+            pltpu.VMEM((ranks, rows * 2 * owned, tokens), F32),
+            pltpu.VMEM((ranks, owned * rows, tokens), BF16),
+            pltpu.VMEM((ranks, owned * rows, tokens), BF16),
+            pltpu.VMEM((ranks, owned * rows, tokens), F32),
+            pltpu.SemaphoreType.DMA((2,)),
+            pltpu.SemaphoreType.DMA((5, ranks)),
+            pltpu.SemaphoreType.DMA((5, ranks)),
+        ],
+        compiler_params=pltpu.CompilerParams(
+            collective_id=0, has_side_effects=True, vmem_limit_bytes=40 * 2**20
+        ),
+    )(
+        jnp.swapaxes(alignment_features, 1, 2),
+        pair_features,
+        token_residue_kind.reshape(1, tokens),
+        alignment_mask.reshape(1, sequences),
+        residue_embedding_table,
+        outer_left_weight.T,
+        outer_right_weight.T,
+        outer_output_weight,
+        averaging_value_weight,
+        averaging_gate_weight,
+        averaging_head_logits.T,
+        averaging_output_weight.T,
+        triangle_projection_weight,
+        triangle_gate_weight,
+        triangle_output_weight,
+    )
+    return jnp.swapaxes(msa_out, 1, 2), pair_out
+
+
 def solution(mesh):
     placed = (
         P(("groups", "row"), None, None),
@@ -143,7 +518,7 @@
         P(),
     )
     return jax.shard_map(
-        local,
+        functools.partial(local, mesh.shape["row"]),
         mesh=mesh,
         in_specs=placed,
         out_specs=(P(("groups", "row"), None, None), P(("groups", "row"), None, None)),

time: 127 us -> 55.6 us (0.44)
  blocking collectives: 64.3 us -> 0 us
  Pallas kernels: 0 us -> 43.5 us
  matrix products: 17.2 us -> 0 us
  waiting for transfers between devices: 15.4 us -> 0 us
  starting transfers between devices: 10.6 us -> 0 us
  local copies, waits for them, and re-layouts: 15.5 us -> 10.7 us
  other arithmetic: 1.67 us -> 0 us
    all_gather x3 -> x0, blocking collectives: 64.3 us -> none  [the longest x1 23.8 us: local(): lax.all_gather(left_projected_rows, 'row', axis=0, tiled=True)]
    pallas_call x0 -> x1, Pallas kernels: none -> 43.5 us  [local(): pl.pallas_call(functools.partial(fused_kernel, ranks), out_shape=(jax.Sha...]
    dot_general x29 -> x0, matrix products: 16.6 us -> none  [the longest x8 7.23 us: outer_block(): summed = jnp.dot(left_row.T, right_flat, preferred_element_type=jnp.float32)]
    all_to_all x3 -> x0, waiting for transfers between devices: 15.4 us -> none  [the longest x1 8.18 us: local(): lax.all_to_all(tri_left, 'row', split_axis=0, concat_axis=1, tiled=True)]
    all_to_all x3 -> x0, starting transfers between devices: 10.6 us -> none  [the longest x1 3.53 us: local(): lax.all_to_all(tri_right, 'row', split_axis=0, concat_axis=1, tiled=True)]
    reshape x10 -> x0, local copies, waits for them, and re-layouts: 7.62 us -> none  [the longest x8 6.37 us: outer_block(): (summed / seq_count).astype(jnp.bfloat16).reshape(width, all_tokens, width)]
    unnamed x28 -> x32, local copies, waits for them, and re-layouts: 4.17 us -> 10.7 us
    convert_element_type x5 -> x0, local copies, waits for them, and re-layouts: 2.8 us -> none  [the longest x1 0.89 us: local(): (jax.nn.sigmoid(projected[3]) * projected[2]).astype(jnp.bfloat16)]
  transfers between devices with their start and end apart: 3 -> 0, of which waited for: 2 -> 0; matrix products, arithmetic and copies ran while one was open for 4% -> 0% of each run, Pallas kernels for 0% -> 0%
where the time goes in v1:
time: 55.6 us; the launch traced here: 54.9 us
  Pallas kernels  43.5 us (78%)
  local copies, waits for them, and re-layouts  10.7 us (19%)
  between operations  0.69 us (1%)
    pallas_call x1, Pallas kernels, local(): pl.pallas_call(functools.partial(fused_kernel, ranks), out_shape=(jax.Sha...  43.5 us
    unnamed x32, local copies, waits for them, and re-layouts  10.7 us

profile of v1, /device:TPU:0, one launch (start us, length us, event | category | flops | bytes accessed | tf_op | source)
XLA Modules:
  0.0 54.9 jit_solution(8720518010509513)
XLA Ops:
  0.6 0.0 copy-start.9
  0.6 0.0 copy-start.12
  0.7 0.0 copy-start.13
  0.7 0.0 copy-start.14
  0.7 0.7 %copy-done.9 = bf16[32,64]{1,0:T(8,128)(2,1)S(1)} copy-done((bf16[32,64]{1,0:T(8,128)(2,1)S(1)}, bf16[32,64]{1,0:T(8,128)(2,1)}, u32[]{:S(2)}) %copy-start.9) | copy-done | bytes 4120
  1.3 0.0 copy-done.12
  1.3 0.0 copy-done.13
  1.3 0.0 copy-done.14
  1.3 0.0 copy-start
  1.3 0.9 %copy-done = bf16[8,128,128]{2,1,0:T(8,128)(2,1)S(1)} copy-done((bf16[8,128,128]{2,1,0:T(8,128)(2,1)S(1)}, bf16[8,128,128]{2,1,0:T(8,128)(2,1)}, u32[]{:S(2)}) %copy-start) | copy-done | bytes 262168
  2.3 0.0 copy-start.1
  2.3 0.9 %copy-done.1 = bf16[1024,128]{1,0:T(8,128)(2,1)S(1)} copy-done((bf16[1024,128]{1,0:T(8,128)(2,1)S(1)}, bf16[1024,128]{1,0:T(8,128)(2,1)}, u32[]{:S(2)}) %copy-start.1) | copy-done | bytes 262168
  3.2 0.9 %copy-done.2 = bf16[128,512]{1,0:T(8,128)(2,1)S(1)} copy-done((bf16[128,512]{1,0:T(8,128)(2,1)S(1)}, bf16[128,512]{1,0:T(8,128)(2,1)}, u32[]{:S(2)}) %copy-start.2) | copy-done | bytes 131096
  4.2 0.8 %copy-done.3 = bf16[2,128,64]{1,2,0:T(8,128)(2,1)S(1)} copy-done((bf16[2,128,64]{1,2,0:T(8,128)(2,1)S(1)}, bf16[2,128,64]{1,2,0:T(8,128)(2,1)}, u32[]{:S(2)}) %copy-start.3) | copy-done | bytes 32792
  4.9 0.8 %copy-done.4 = bf16[64,256]{1,0:T(8,128)(2,1)S(1)} copy-done((bf16[64,256]{1,0:T(8,128)(2,1)S(1)}, bf16[64,256]{1,0:T(8,128)(2,1)}, u32[]{:S(2)}) %copy-start.4) | copy-done | bytes 32792
  5.7 0.8 %copy-done.5 = bf16[64,256]{1,0:T(8,128)(2,1)S(1)} copy-done((bf16[64,256]{1,0:T(8,128)(2,1)S(1)}, bf16[64,256]{1,0:T(8,128)(2,1)}, u32[]{:S(2)}) %copy-start.5) | copy-done | bytes 32792
  6.4 0.8 %copy-done.6 = bf16[256,64]{0,1:T(8,128)(2,1)S(1)} copy-done((bf16[256,64]{0,1:T(8,128)(2,1)S(1)}, bf16[256,64]{0,1:T(8,128)(2,1)}, u32[]{:S(2)}) %copy-start.6) | copy-done | bytes 32792
  7.2 0.8 %copy-done.7 = bf16[128,128]{1,0:T(8,128)(2,1)S(1)} copy-done((bf16[128,128]{1,0:T(8,128)(2,1)S(1)}, bf16[128,128]{1,0:T(8,128)(2,1)}, u32[]{:S(2)}) %copy-start.7) | copy-done | bytes 32792
  7.9 0.8 %copy-done.8 = bf16[128,128]{1,0:T(8,128)(2,1)S(1)} copy-done((bf16[128,128]{1,0:T(8,128)(2,1)S(1)}, bf16[128,128]{1,0:T(8,128)(2,1)}, u32[]{:S(2)}) %copy-start.8) | copy-done | bytes 32792
  8.7 0.7 %copy-done.10 = bf16[64,32]{0,1:T(8,128)(2,1)S(1)} copy-done((bf16[64,32]{0,1:T(8,128)(2,1)S(1)}, bf16[64,32]{0,1:T(8,128)(2,1)}, u32[]{:S(2)}) %copy-start.10) | copy-done | bytes 4120
  9.4 0.7 %copy-done.11 = bf16[64,32]{0,1:T(8,128)(2,1)S(1)} copy-done((bf16[64,32]{0,1:T(8,128)(2,1)S(1)}, bf16[64,32]{0,1:T(8,128)(2,1)}, u32[]{:S(2)}) %copy-start.11) | copy-done | bytes 4120
  10.1 43.5 %shard_map.158 = (bf16[2,64,128]{2,1,0:T(8,128)(2,1)S(1)}, bf16[8,128,128]{2,1,0:T(8,128)(2,1)S(1)}) custom-call(bf16[2,64,128]{2,1,0:T(8,128)(2,1)S(1)} %bitcast.9, bf16[8,128,128]{2,1,0:T(8,128)(2,1)S(1)} %copy-done, s32[1,128]{1,0:T(1,128)S(1)} %bitcast.14, s32[1,32]{1,0:T(1,128)S(1)} %bitcast.15, bf16[32,64]{1,0:T(8,128)(2,1)S(1)} %copy-done.9, ...), custom_call_target="tpu_custom_call" | custom-call | tf_op jit(solution)/shard_map/pallas_call | solution.py:447
  53.6 0.6 %copy.19 = bf16[2,128,64]{1,2,0:T(8,128)(2,1)} copy(bf16[2,128,64]{1,2,0:T(8,128)(2,1)S(1)} %bitcast.8) | data formatting | bytes 65536
  54.2 0.7 %copy.20 = bf16[8,128,128]{2,1,0:T(8,128)(2,1)} copy(bf16[8,128,128]{2,1,0:T(8,128)(2,1)S(1)} %get-tuple-element.9) | data formatting | bytes 524288
  (9 shorter events, 0.0 us)
Async XLA Ops:
  0.6 0.7 %copy-start.9 = (bf16[32,64]{1,0:T(8,128)(2,1)S(1)}, bf16[32,64]{1,0:T(8,128)(2,1)}, u32[]{:S(2)}) copy-start(bf16[32,64]{1,0:T(8,128)(2,1)} %table_ref.1) | copy-start | bytes 12292
  0.6 0.7 %copy-start.12 = (bf16[128,8]{0,1:T(8,128)(2,1)S(1)}, bf16[128,8]{0,1:T(8,128)(2,1)}, u32[]{:S(2)}) copy-start(bf16[128,8]{0,1:T(8,128)(2,1)} %param.25) | copy-start | bytes 6148
  0.7 0.7 %copy-start.13 = (s32[128]{0:T(128)S(1)}, s32[128]{0:T(128)}, u32[]{:S(2)}) copy-start(s32[128]{0:T(128)} %param.17) | copy-start | bytes 1540
  0.7 0.7 %copy-start.14 = (s32[32]{0:T(128)S(1)}, s32[32]{0:T(128)}, u32[]{:S(2)}) copy-start(s32[32]{0:T(128)} %param.18) | copy-start | bytes 388
  1.3 1.0 %copy-start = (bf16[8,128,128]{2,1,0:T(8,128)(2,1)S(1)}, bf16[8,128,128]{2,1,0:T(8,128)(2,1)}, u32[]{:S(2)}) copy-start(bf16[8,128,128]{2,1,0:T(8,128)(2,1)} %pair_hbm.1) | copy-start | bytes 786436
  2.3 0.9 %copy-start.1 = (bf16[1024,128]{1,0:T(8,128)(2,1)S(1)}, bf16[1024,128]{1,0:T(8,128)(2,1)}, u32[]{:S(2)}) copy-start(bf16[1024,128]{1,0:T(8,128)(2,1)} %outer_w_hbm.1) | copy-start | bytes 786436
  3.2 0.9 %copy-start.2 = (bf16[128,512]{1,0:T(8,128)(2,1)S(1)}, bf16[128,512]{1,0:T(8,128)(2,1)}, u32[]{:S(2)}) copy-start(bf16[128,512]{1,0:T(8,128)(2,1)} %tri_w_ref.1) | copy-start | bytes 393220
  4.1 0.8 %copy-start.3 = (bf16[2,128,64]{1,2,0:T(8,128)(2,1)S(1)}, bf16[2,128,64]{1,2,0:T(8,128)(2,1)}, u32[]{:S(2)}) copy-start(bf16[2,128,64]{1,2,0:T(8,128)(2,1)} %param.15) | copy-start | bytes 98308
  4.9 0.8 %copy-start.4 = (bf16[64,256]{1,0:T(8,128)(2,1)S(1)}, bf16[64,256]{1,0:T(8,128)(2,1)}, u32[]{:S(2)}) copy-start(bf16[64,256]{1,0:T(8,128)(2,1)} %value_w_ref.1) | copy-start | bytes 98308
  5.7 0.8 %copy-start.5 = (bf16[64,256]{1,0:T(8,128)(2,1)S(1)}, bf16[64,256]{1,0:T(8,128)(2,1)}, u32[]{:S(2)}) copy-start(bf16[64,256]{1,0:T(8,128)(2,1)} %gate_w_ref.1) | copy-start | bytes 98308
  6.4 0.8 %copy-start.6 = (bf16[256,64]{0,1:T(8,128)(2,1)S(1)}, bf16[256,64]{0,1:T(8,128)(2,1)}, u32[]{:S(2)}) copy-start(bf16[256,64]{0,1:T(8,128)(2,1)} %param.26) | copy-start | bytes 98308
  7.2 0.8 %copy-start.7 = (bf16[128,128]{1,0:T(8,128)(2,1)S(1)}, bf16[128,128]{1,0:T(8,128)(2,1)}, u32[]{:S(2)}) copy-start(bf16[128,128]{1,0:T(8,128)(2,1)} %tri_gate_w_ref.1) | copy-start | bytes 98308
  7.9 0.8 %copy-start.8 = (bf16[128,128]{1,0:T(8,128)(2,1)S(1)}, bf16[128,128]{1,0:T(8,128)(2,1)}, u32[]{:S(2)}) copy-start(bf16[128,128]{1,0:T(8,128)(2,1)} %tri_out_w_ref.1) | copy-start | bytes 98308
  8.7 0.7 %copy-start.10 = (bf16[64,32]{0,1:T(8,128)(2,1)S(1)}, bf16[64,32]{0,1:T(8,128)(2,1)}, u32[]{:S(2)}) copy-start(bf16[64,32]{0,1:T(8,128)(2,1)} %param.20) | copy-start | bytes 12292
  9.4 0.7 %copy-start.11 = (bf16[64,32]{0,1:T(8,128)(2,1)S(1)}, bf16[64,32]{0,1:T(8,128)(2,1)}, u32[]{:S(2)}) copy-start(bf16[64,32]{0,1:T(8,128)(2,1)} %param.21) | copy-start | bytes 12292

commit v2 on v1

--- a/solution.py
+++ b/solution.py
@@ -130,6 +130,8 @@
 
 F32 = jnp.float32
 BF16 = jnp.bfloat16
+PLANE = 4
+CHUNK = 2
 
 
 def matmul(a, b, dim_a, dim_b):
@@ -138,14 +140,31 @@
 
 def fused_kernel(
     ranks,
+    msa_hbm,
+    pair_hbm,
+    kind_hbm,
+    mask_hbm,
+    table_hbm,
+    left_w_hbm,
+    right_w_hbm,
+    outer_w_hbm,
+    value_w_hbm,
+    gate_w_hbm,
+    head_w_hbm,
+    average_w_hbm,
+    tri_w_hbm,
+    tri_gate_w_hbm,
+    tri_out_w_hbm,
+    msa_out_ref,
+    pair_out_ref,
     msa_ref,
-    pair_hbm,
+    pair_ref,
     kind_ref,
     mask_ref,
     table_ref,
     left_w_ref,
     right_w_ref,
-    outer_w_hbm,
+    outer_w_ref,
     value_w_ref,
     gate_w_ref,
     head_w_ref,
@@ -153,10 +172,6 @@
     tri_w_ref,
     tri_gate_w_ref,
     tri_out_w_ref,
-    msa_out_ref,
-    pair_out_ref,
-    pair_ref,
-    outer_w_ref,
     outer_f32,
     left_send,
     left_buf,
@@ -189,10 +204,46 @@
     head_dim = value_w_ref.shape[1] // heads
     sequences = seqs * ranks
 
-    load_pair = pltpu.make_async_copy(pair_hbm, pair_ref, local_sem.at[0])
-    load_outer = pltpu.make_async_copy(outer_w_hbm, outer_w_ref, local_sem.at[1])
-    load_outer.start()
-    load_pair.start()
+    sources = (
+        msa_hbm,
+        pair_hbm,
+        kind_hbm,
+        mask_hbm,
+        table_hbm,
+        left_w_hbm,
+        right_w_hbm,
+        outer_w_hbm,
+        value_w_hbm,
+        gate_w_hbm,
+        head_w_hbm,
+        average_w_hbm,
+        tri_w_hbm,
+        tri_gate_w_hbm,
+        tri_out_w_hbm,
+    )
+    targets = (
+        msa_ref,
+        pair_ref,
+        kind_ref,
+        mask_ref,
+        table_ref,
+        left_w_ref,
+        right_w_ref,
+        outer_w_ref,
+        value_w_ref,
+        gate_w_ref,
+        head_w_ref,
+        average_w_ref,
+        tri_w_ref,
+        tri_gate_w_ref,
+        tri_out_w_ref,
+    )
+    loads = [
+        pltpu.make_async_copy(source, target, local_sem.at[n])
+        for n, (source, target) in enumerate(zip(sources, targets))
+    ]
+    for n in (0, 2, 3, 4, 5, 6, 7, 12, 8, 9, 1, 10, 11, 13, 14):
+        loads[n].start()
 
     barrier = pltpu.get_barrier_semaphore()
 
@@ -207,11 +258,11 @@
 
     lax.fori_loop(1, ranks, greet, 0)
 
-    def remote(phase, step, source, target):
+    def exchange(phase, step, source, target):
         peer = lax.rem(me + step, ranks)
         return pltpu.make_async_remote_copy(
-            src_ref=source.at[peer] if source is not target else source.at[me],
-            dst_ref=target.at[me],
+            src_ref=source(peer),
+            dst_ref=target(me),
             send_sem=send_sem.at[phase, step],
             recv_sem=recv_sem.at[phase, step],
             device_id={"row": peer},
@@ -220,28 +271,80 @@
 
     def send_all(phase, source, target):
         def body(step, carry):
-            remote(phase, step, source, target).start()
+            exchange(phase, step, source, target).start()
             return carry
 
         lax.fori_loop(1, ranks, body, 0)
 
-    def receive_all(phase, source, target, wide):
+    def receive_all(phase, source, target, arrived):
         def body(step, carry):
-            remote(phase, step, source, target).wait_recv()
-            if wide is not None:
-                origin = lax.rem(me - step + ranks, ranks)
-                wide[origin] = target[origin].astype(F32).reshape(wide.shape[1:])
+            exchange(phase, step, source, target).wait_recv()
+            arrived(lax.rem(me - step + ranks, ranks))
             return carry
 
         lax.fori_loop(1, ranks, body, 0)
 
     def drain(phase, source, target):
         def body(step, carry):
-            remote(phase, step, source, target).wait_send()
+            exchange(phase, step, source, target).wait_send()
             return carry
 
         lax.fori_loop(1, ranks, body, 0)
 
+    planes = ranks // PLANE
+    my_plane = me // PLANE
+    place = lax.rem(me, PLANE)
+
+    def origin_of(far, near):
+        plane = lax.rem(my_plane - far + planes, planes)
+        return plane * PLANE + lax.rem(place - near + PLANE, PLANE)
+
+    def gather(phase, far, near, buffer):
+        if near == 0:
+            peer = lax.rem(my_plane + far, planes) * PLANE + place
+            block = me
+        else:
+            peer = my_plane * PLANE + lax.rem(place + near, PLANE)
+            block = origin_of(far, 0)
+        return pltpu.make_async_remote_copy(
+            src_ref=buffer.at[block],
+            dst_ref=buffer.at[block],
+            send_sem=send_sem.at[phase, far * PLANE + near],
+            recv_sem=recv_sem.at[phase, far * PLANE + near],
+            device_id={"row": peer},
+            device_id_type=pl.DeviceIdType.MESH,
+        )
+
+    def gather_start(phase, buffer):
+        for far in range(1, planes):
+            gather(phase, far, 0, buffer).start()
+        for near in range(1, PLANE):
+            gather(phase, 0, near, buffer).start()
+
+    def gather_forward(phase, buffer):
+        for far in range(1, planes):
+            gather(phase, far, 0, buffer).wait_recv()
+            for near in range(1, PLANE):
+                gather(phase, far, near, buffer).start()
+
+    def gather_finish(phase, buffer, wide):
+        wide[me] = buffer[me].astype(F32)
+        for far in range(1, planes):
+            wide[origin_of(far, 0)] = buffer[origin_of(far, 0)].astype(F32)
+        for far in range(planes):
+            for near in range(1, PLANE):
+                gather(phase, far, near, buffer).wait_recv()
+                wide[origin_of(far, near)] = buffer[origin_of(far, near)].astype(F32)
+
+    def gather_drain(phase, buffer):
+        for step in range(1, ranks):
+            gather(phase, step // PLANE, step % PLANE, buffer).wait_send()
+
+    def piece(ref, chunk):
+        return lambda rank: ref.at[rank, chunk * CHUNK : (chunk + 1) * CHUNK]
+
+    for n in (0, 2, 3, 4, 5, 6):
+        loads[n].wait()
     classes = table_ref.shape[0]
     one_hot = jnp.where(
         lax.broadcasted_iota(jnp.int32, (classes, tokens), 0) == kind_ref[...], 1.0, 0.0
@@ -270,12 +373,13 @@
     left_send[...] = left_turned.reshape(ranks, rows, 128)
 
     pl.semaphore_wait(barrier, ranks - 1)
-    send_all(0, right_buf, right_buf)
-    send_all(1, left_send, left_buf)
+    gather_start(0, right_buf)
+    left_refs = (lambda rank: left_send.at[rank], lambda rank: left_buf.at[rank])
+    send_all(1, *left_refs)
 
     left_buf[me] = left_send[me]
-    right_f32[me] = right_buf[me].astype(F32)
-    load_outer.wait()
+    for n in (7, 12, 8, 9):
+        loads[n].wait()
     outer_f32[...] = outer_w_ref[...].astype(F32)
     turned = tri_w_ref[...].astype(F32).T
     blocks = [
@@ -288,7 +392,8 @@
     values = matmul(value_w_ref[...], msa_normed, 0, 0).astype(BF16)
     gates = jax.nn.sigmoid(matmul(gate_w_ref[...], msa_normed, 0, 0))
 
-    receive_all(1, left_send, left_buf, None)
+    gather_forward(0, right_buf)
+    receive_all(1, *left_refs, lambda origin: None)
     left_lane = lax.broadcasted_iota(jnp.int32, (ranks, seqs * width), 1)
     left_parts = []
     for i in range(rows):
@@ -313,14 +418,15 @@
                     n * pair_channels : (n + 1) * pair_channels,
                 ]
 
-    receive_all(0, right_buf, right_buf, right_f32)
+    gather_finish(0, right_buf, right_f32)
     right_flat = right_f32.reshape(ranks * seqs * width, tokens)
     for b in range(width):
         parts = [
             right_flat[pl.ds(s * width + b, ranks, stride=seqs * width), :] for s in range(seqs)
         ]
         right_all[b * sequences : (b + 1) * sequences] = jnp.concatenate(parts, axis=0).astype(BF16)
-    load_pair.wait()
+    for n in (1, 10, 11, 13, 14):
+        loads[n].wait()
     scale = 1.0 / seq_count
     right_turned = right_all[...].T
     for i in range(0, rows, 2):
@@ -342,8 +448,10 @@
             tri_send[:, i + n] = gated[:, n * tokens : (n + 1) * tokens].reshape(
                 ranks, 2 * owned, tokens
             )
-    send_all(2, tri_send, tri_buf)
-
+        chunk = i // CHUNK
+        send_all(2 + chunk, piece(tri_send, chunk), piece(tri_buf, chunk))
+
+    last = 2 + rows // CHUNK - 1
     pair_normed = pair_normed_ref[...].reshape(rows * tokens, pair_channels)
     logits = matmul(head_w_ref[...], pair_normed, 1, 1)
     logits = jnp.concatenate(
@@ -351,13 +459,21 @@
     )
     powers = jnp.exp(logits - jnp.max(logits, axis=1, keepdims=True))
     weight_buf[me] = (powers / jnp.sum(powers, axis=1, keepdims=True)).astype(BF16)
-    send_all(3, weight_buf, weight_buf)
-    weight_f32[me] = weight_buf[me].astype(F32)
-    tri_buf[me] = tri_send[me]
+    gather_start(1 + last, weight_buf)
     tri_f32[me] = tri_send[me].astype(F32).reshape(tri_f32.shape[1:])
     tri_gate = jax.nn.sigmoid(matmul(pair_normed, tri_gate_w_ref[...], 1, 0))
 
-    receive_all(2, tri_send, tri_buf, tri_f32)
+    for chunk in range(rows // CHUNK):
+        part = 2 * owned * CHUNK
+
+        def widen(origin, chunk=chunk, part=part):
+            tri_f32[origin, chunk * part : (chunk + 1) * part] = (
+                tri_buf[origin, chunk * CHUNK : (chunk + 1) * CHUNK]
+                .astype(F32)
+                .reshape(part, tokens)
+            )
+
+        receive_all(2 + chunk, piece(tri_send, chunk), piece(tri_buf, chunk), widen)
     tri_flat = tri_f32.reshape(ranks * rows * 2 * owned, tokens)
     sums = []
     for c in range(owned):
@@ -370,11 +486,12 @@
             back_send[:, (c - 1) * rows : (c + 1) * rows] = jnp.concatenate(
                 sums[-2:], axis=1
             ).astype(BF16)
-    send_all(4, back_send, back_buf)
-    back_buf[me] = back_send[me]
+    back = (lambda rank: back_send.at[rank], lambda rank: back_buf.at[rank])
+    send_all(2 + last, *back)
+    gather_forward(1 + last, weight_buf)
     back_f32[me] = back_send[me].astype(F32)
 
-    receive_all(3, weight_buf, weight_buf, weight_f32)
+    gather_finish(1 + last, weight_buf, weight_f32)
     weight_flat = weight_f32.reshape(ranks * rows * heads, tokens)
     averaged = [[] for _ in range(seqs)]
     for h in range(heads):
@@ -396,7 +513,11 @@
             starts[s].astype(F32) + update[:, s * tokens : (s + 1) * tokens]
         ).astype(BF16)
 
-    receive_all(4, back_send, back_buf, back_f32)
+
+    def widen_back(origin):
+        back_f32[origin] = back_buf[origin].astype(F32)
+
+    receive_all(2 + last, *back, widen_back)
     back_flat = back_f32.reshape(tri_channels * rows, tokens)
     for i in range(rows):
         one = back_flat[pl.ds(i, tri_channels, stride=rows), :]
@@ -405,11 +526,12 @@
         pair_out_ref[i] = (
             pair_mid_ref[i].astype(F32) + tri_gate[i * tokens : (i + 1) * tokens] * update
         ).astype(BF16)
-    drain(0, right_buf, right_buf)
-    drain(1, left_send, left_buf)
-    drain(2, tri_send, tri_buf)
-    drain(3, weight_buf, weight_buf)
-    drain(4, back_send, back_buf)
+    gather_drain(0, right_buf)
+    drain(1, *left_refs)
+    for chunk in range(rows // CHUNK):
+        drain(2 + chunk, piece(tri_send, chunk), piece(tri_buf, chunk))
+    gather_drain(1 + last, weight_buf)
+    drain(2 + last, *back)
 
 
 def local(ranks, *arguments):
@@ -436,25 +558,37 @@
     width = outer_left_weight.shape[1]
     heads = averaging_head_logits.shape[1]
     owned = tri_channels // ranks
-    if (2 * owned) % 16 or rows != 8 or heads != 8 or (seqs * ranks) % 16 or seqs * width > 128:
+    if (2 * owned) % 16 or rows != 8 or heads != 8 or (seqs * ranks) % 16 or seqs * width > 128 or ranks % PLANE:
         return local_large(*arguments)
     sequences = seqs * ranks
     vmem = pl.BlockSpec(memory_space=pltpu.VMEM)
-    hbm = pl.BlockSpec(memory_space=pl.ANY)
-    in_specs = [vmem] * 15
-    in_specs[1] = hbm
-    in_specs[7] = hbm
+    operands = (
+        jnp.swapaxes(alignment_features, 1, 2),
+        pair_features,
+        token_residue_kind.reshape(1, tokens),
+        alignment_mask.reshape(1, sequences),
+        residue_embedding_table,
+        outer_left_weight.T,
+        outer_right_weight.T,
+        outer_output_weight,
+        averaging_value_weight,
+        averaging_gate_weight,
+        averaging_head_logits.T,
+        averaging_output_weight.T,
+        triangle_projection_weight,
+        triangle_gate_weight,
+        triangle_output_weight,
+    )
     msa_out, pair_out = pl.pallas_call(
         functools.partial(fused_kernel, ranks),
         out_shape=(
             jax.ShapeDtypeStruct((seqs, channels, tokens), BF16),
             jax.ShapeDtypeStruct((rows, tokens, pair_channels), BF16),
         ),
-        in_specs=in_specs,
+        in_specs=[pl.BlockSpec(memory_space=pl.ANY)] * len(operands),
         out_specs=(vmem, vmem),
         scratch_shapes=[
-            pltpu.VMEM((rows, tokens, pair_channels), BF16),
-            pltpu.VMEM((width * width, pair_channels), BF16),
+            *[pltpu.VMEM(operand.shape, operand.dtype) for operand in operands],
             pltpu.VMEM((width * width, pair_channels), F32),
             pltpu.VMEM((ranks, rows, 128), F32),
             pltpu.VMEM((ranks, rows, 128), F32),
@@ -472,30 +606,14 @@
             pltpu.VMEM((ranks, owned * rows, tokens), BF16),
             pltpu.VMEM((ranks, owned * rows, tokens), BF16),
             pltpu.VMEM((ranks, owned * rows, tokens), F32),
-            pltpu.SemaphoreType.DMA((2,)),
-            pltpu.SemaphoreType.DMA((5, ranks)),
-            pltpu.SemaphoreType.DMA((5, ranks)),
+            pltpu.SemaphoreType.DMA((len(operands),)),
+            pltpu.SemaphoreType.DMA((4 + rows // CHUNK, ranks)),
+            pltpu.SemaphoreType.DMA((4 + rows // CHUNK, ranks)),
         ],
         compiler_params=pltpu.CompilerParams(
-            collective_id=0, has_side_effects=True, vmem_limit_bytes=40 * 2**20
+            collective_id=0, has_side_effects=True, vmem_limit_bytes=60 * 2**20
         ),
-    )(
-        jnp.swapaxes(alignment_features, 1, 2),
-        pair_features,
-        token_residue_kind.reshape(1, tokens),
-        alignment_mask.reshape(1, sequences),
-        residue_embedding_table,
-        outer_left_weight.T,
-        outer_right_weight.T,
-        outer_output_weight,
-        averaging_value_weight,
-        averaging_gate_weight,
-        averaging_head_logits.T,
-        averaging_output_weight.T,
-        triangle_projection_weight,
-        triangle_gate_weight,
-        triangle_output_weight,
-    )
+    )(*operands)
     return jnp.swapaxes(msa_out, 1, 2), pair_out
 
 

time: 55.6 us -> 43.9 us (0.79)
  local copies, waits for them, and re-layouts: 10.7 us -> 3.05 us
  Pallas kernels: 43.5 us -> 40 us
    unnamed x32 -> x2, local copies, waits for them, and re-layouts: 10.7 us -> 3.05 us
    pallas_call x1, Pallas kernels: 43.5 us -> 40 us  [local(): pl.pallas_call(functools.partial(fused_kernel, ranks), out_shape=(jax.Sha...]
where the time goes in v2:
time: 43.9 us; the launch traced here: 43.7 us
  Pallas kernels  40 us (91%)
  local copies, waits for them, and re-layouts  3.05 us (7%)
  between operations  0.64 us (1%)
    pallas_call x1, Pallas kernels, local(): pl.pallas_call(functools.partial(fused_kernel, ranks), out_shape=(jax.Sha...  40 us
    unnamed x2, local copies, waits for them, and re-layouts  3.05 us

profile of v2, /device:TPU:0, one launch (start us, length us, event | category | flops | bytes accessed | tf_op | source)
XLA Modules:
  0.0 43.7 jit_solution(14695510732985896946)
XLA Ops:
  0.6 40.0 %shard_map.158 = (bf16[2,64,128]{2,1,0:T(8,128)(2,1)}, bf16[8,128,128]{2,1,0:T(8,128)(2,1)}) custom-call(bf16[2,64,128]{2,1,0:T(8,128)(2,1)} %bitcast.9, bf16[8,128,128]{2,1,0:T(8,128)(2,1)} %pair_hbm.1, s32[1,128]{1,0:T(1,128)} %bitcast.14, s32[1,32]{1,0:T(1,128)} %bitcast.15, bf16[32,64]{1,0:T(8,128)(2,1)} %table_hbm.1, bf16[32,64]{1,0:T(8,128)(2,1)} %bitcast.11, ...), custom_call_target="tpu_custom_call" | custom-call | tf_op jit(solution)/shard_map/pallas_call | solution.py:582
  40.6 1.4 %copy.19 = bf16[2,128,64]{1,2,0:T(8,128)(2,1)} copy(bf16[2,128,64]{1,2,0:T(8,128)(2,1)} %bitcast.8) | data formatting | bytes 65536
  42.0 1.7 %copy.20 = bf16[8,128,128]{2,1,0:T(8,128)(2,1)} copy(bf16[8,128,128]{2,1,0:T(8,128)(2,1)} %get-tuple-element.9) | data formatting | bytes 524288

commit v3 on v2

--- a/solution.py
+++ b/solution.py
@@ -131,7 +131,7 @@
 F32 = jnp.float32
 BF16 = jnp.bfloat16
 PLANE = 4
-CHUNK = 2
+CHUNK = 8
 
 
 def matmul(a, b, dim_a, dim_b):
@@ -448,8 +448,9 @@
             tri_send[:, i + n] = gated[:, n * tokens : (n + 1) * tokens].reshape(
                 ranks, 2 * owned, tokens
             )
-        chunk = i // CHUNK
-        send_all(2 + chunk, piece(tri_send, chunk), piece(tri_buf, chunk))
+        if (i + 2) % CHUNK == 0:
+            chunk = i // CHUNK
+            send_all(2 + chunk, piece(tri_send, chunk), piece(tri_buf, chunk))
 
     last = 2 + rows // CHUNK - 1
     pair_normed = pair_normed_ref[...].reshape(rows * tokens, pair_channels)

time: 43.9 us -> 41.2 us (0.938)
  Pallas kernels: 40 us -> 37.3 us
    pallas_call x1, Pallas kernels: 40 us -> 37.3 us  [local(): pl.pallas_call(functools.partial(fused_kernel, ranks), out_shape=(jax.Sha...]
where the time goes in v3:
time: 41.2 us; the launch traced here: 41 us
  Pallas kernels  37.3 us (91%)
  local copies, waits for them, and re-layouts  3.05 us (7%)
  between operations  0.64 us (2%)
    pallas_call x1, Pallas kernels, local(): pl.pallas_call(functools.partial(fused_kernel, ranks), out_shape=(jax.Sha...  37.3 us
    unnamed x2, local copies, waits for them, and re-layouts  3.05 us

profile of v3, /device:TPU:0, one launch (start us, length us, event | category | flops | bytes accessed | tf_op | source)
XLA Modules:
  0.0 41.0 jit_solution(5605819765159832187)
XLA Ops:
  0.6 37.3 %shard_map.158 = (bf16[2,64,128]{2,1,0:T(8,128)(2,1)}, bf16[8,128,128]{2,1,0:T(8,128)(2,1)}) custom-call(bf16[2,64,128]{2,1,0:T(8,128)(2,1)} %bitcast.9, bf16[8,128,128]{2,1,0:T(8,128)(2,1)} %pair_hbm.1, s32[1,128]{1,0:T(1,128)} %bitcast.14, s32[1,32]{1,0:T(1,128)} %bitcast.15, bf16[32,64]{1,0:T(8,128)(2,1)} %table_hbm.1, bf16[32,64]{1,0:T(8,128)(2,1)} %bitcast.11, ...), custom_call_target="tpu_custom_call" | custom-call | tf_op jit(solution)/shard_map/pallas_call | solution.py:583
  38.0 1.4 %copy.19 = bf16[2,128,64]{1,2,0:T(8,128)(2,1)} copy(bf16[2,128,64]{1,2,0:T(8,128)(2,1)} %bitcast.8) | data formatting | bytes 65536
  39.3 1.7 %copy.20 = bf16[8,128,128]{2,1,0:T(8,128)(2,1)} copy(bf16[8,128,128]{2,1,0:T(8,128)(2,1)} %get-tuple-element.9) | data formatting | bytes 524288

commit v4 on v3

--- a/solution.py
+++ b/solution.py
@@ -274,7 +274,7 @@
             exchange(phase, step, source, target).start()
             return carry
 
-        lax.fori_loop(1, ranks, body, 0)
+        lax.fori_loop(1, ranks, body, 0, unroll=True)
 
     def receive_all(phase, source, target, arrived):
         def body(step, carry):
@@ -282,14 +282,14 @@
             arrived(lax.rem(me - step + ranks, ranks))
             return carry
 
-        lax.fori_loop(1, ranks, body, 0)
+        lax.fori_loop(1, ranks, body, 0, unroll=True)
 
     def drain(phase, source, target):
         def body(step, carry):
             exchange(phase, step, source, target).wait_send()
             return carry
 
-        lax.fori_loop(1, ranks, body, 0)
+        lax.fori_loop(1, ranks, body, 0, unroll=True)
 
     planes = ranks // PLANE
     my_plane = me // PLANE

time: 41.2 us -> 40.9 us (level)
  no operation moved by 1% of the time
where the time goes in v4:
time: 40.9 us; the launch traced here: 40.6 us
  Pallas kernels  36.9 us (90%)
  local copies, waits for them, and re-layouts  3.05 us (7%)
  between operations  0.64 us (2%)
    pallas_call x1, Pallas kernels, local(): pl.pallas_call(functools.partial(fused_kernel, ranks), out_shape=(jax.Sha...  36.9 us
    unnamed x2, local copies, waits for them, and re-layouts  3.05 us

profile of v4, /device:TPU:0, one launch (start us, length us, event | category | flops | bytes accessed | tf_op | source)
XLA Modules:
  0.0 40.6 jit_solution(12256966847530450873)
XLA Ops:
  0.6 36.9 %shard_map.158 = (bf16[2,64,128]{2,1,0:T(8,128)(2,1)}, bf16[8,128,128]{2,1,0:T(8,128)(2,1)}) custom-call(bf16[2,64,128]{2,1,0:T(8,128)(2,1)} %bitcast.9, bf16[8,128,128]{2,1,0:T(8,128)(2,1)} %pair_hbm.1, s32[1,128]{1,0:T(1,128)} %bitcast.14, s32[1,32]{1,0:T(1,128)} %bitcast.15, bf16[32,64]{1,0:T(8,128)(2,1)} %table_hbm.1, bf16[32,64]{1,0:T(8,128)(2,1)} %bitcast.11, ...), custom_call_target="tpu_custom_call" | custom-call | tf_op jit(solution)/shard_map/pallas_call | solution.py:583
  37.6 1.4 %copy.19 = bf16[2,128,64]{1,2,0:T(8,128)(2,1)} copy(bf16[2,128,64]{1,2,0:T(8,128)(2,1)} %bitcast.8) | data formatting | bytes 65536
  39.0 1.7 %copy.20 = bf16[8,128,128]{2,1,0:T(8,128)(2,1)} copy(bf16[8,128,128]{2,1,0:T(8,128)(2,1)} %get-tuple-element.9) | data formatting | bytes 524288
